TPU v7x, 512 devices: a whole 4x4x16 slice. The times are simulated.
512 devices in a mesh: rep: 32 (over y, x, core), shard: 16 (over z).
Axes of the slice: x: 4, y: 4, z: 16, core: 2. Of those that a mesh axis runs over, the one named last changes fastest.
Arguments:
- activations: bfloat16 [32, 2048, 4096], P('rep', None, 'shard'), may hold values from -6 to 6
- output_grad: bfloat16 [32, 2048, 1664], P('rep', 'shard'), may hold values from -0.125 to 0.125
- feedback: bfloat16 [32, 4096, 1664], P('rep', 'shard'), may hold values from -4 to 4
- right_start: float32 [1664, 32], replicated, may hold values from -6 to 6
Outputs:
- averaged: bfloat16 [4096, 1664], P('shard')
- feedback_next: bfloat16 [32, 4096, 1664], P('rep', 'shard')
- right_factor: float32 [1664, 32], replicated
All inputs are finite; a program needn't handle non-finite values.
Results may differ from a plain program's by a relative error of at most 0.0013.
Values may be sent and summed in bfloat16 or wider, within the bound.
A program may use at most 64 MiB of HBM per device.

v0:
```python
import jax
import jax.numpy as jnp
from jax import lax
from jax.sharding import PartitionSpec as P


def add_outer(activations_local, piece):
    return lax.dot_general(
        activations_local, piece, (((0,), (0,)), ((), ())), preferred_element_type=jnp.float32
    )


def orthonormalize(projected, gram_matrix):
    cholesky_factor = jnp.linalg.cholesky(gram_matrix)
    return jax.scipy.linalg.solve_triangular(cholesky_factor, projected.T, lower=True).T


def on_device(activations, output_grad, feedback, right_start):
    highest = lax.Precision.HIGHEST
    local_acts = activations[0]
    carried = feedback[0].astype(jnp.float32)
    local_grad = output_grad[0]
    merged = (
        add_outer(local_acts, lax.all_gather(local_grad, "shard", axis=0, tiled=True)) + carried
    )
    partial_proj = jnp.dot(
        merged, right_start, precision=highest, preferred_element_type=jnp.float32
    )
    projected = lax.psum(partial_proj, "rep")
    gram_part = jnp.dot(
        projected.T, projected, precision=highest, preferred_element_type=jnp.float32
    )
    gram_matrix = lax.psum(gram_part, "shard")
    orthonormal = orthonormalize(projected, gram_matrix)
    right_part = lax.dot_general(
        merged,
        orthonormal,
        (((0,), (0,)), ((), ())),
        precision=highest,
        preferred_element_type=jnp.float32,
    )
    right_factor = lax.psum(right_part, ("rep", "shard")) / lax.axis_size("rep")
    rebuilt = jnp.dot(
        orthonormal, right_factor.T, precision=highest, preferred_element_type=jnp.float32
    )
    averaged = rebuilt.astype(jnp.bfloat16)
    feedback_next = (merged - rebuilt)[None].astype(jnp.bfloat16)
    return (averaged, feedback_next, right_factor)


def solution(mesh):
    return jax.shard_map(
        on_device,
        mesh=mesh,
        in_specs=(P("rep", None, "shard"), P("rep", "shard", None), P("rep", "shard", None), P()),
        out_specs=(P("shard", None), P("rep", "shard", None), P()),
        check_vma=False,
    )
```

profile of v0, /device:TPU:1, one launch (start us, length us, event | category | flops | bytes accessed | tf_op | source)
XLA Modules:
  0.0 763.2 jit_solution(2582085349503233600)
XLA Ops:
  7.2 0.0 copy-start
  7.2 0.0 all-gather.3.cloned.1.call-start
  7.2 0.7 all-gather.3.cloned.1.call-update
  7.9 0.0 copy-start.2
  7.9 0.0 all-reduce.2.cloned.1.call-start
  8.0 97.5 %all-gather.3.cloned.1.call-done = bf16[1,2048,1664]{2,1,0:T(8,128)(2,1)} async-done(((bf16[1,128,1664]{2,1,0:T(8,128)(2,1)}), bf16[1,2048,1664]{2,1,0:T(8,128)(2,1)}) %all-gather.3.cloned.1.call-update) | async-done | bytes 6815760 | tf_op jit(solution)/shard_map/all_gather | solution.py:24
  105.4 0.0 copy-done
  105.4 5.2 fusion.2
  110.6 0.0 copy-done.2
  110.6 1.5 fusion.11
  112.2 123.1 %psum.21 = f32[256,32]{0,1:T(8,128)S(1)} all-reduce(f32[256,32]{0,1:T(8,128)S(1)} %fusion.11), channel_id=1, replica_groups=mesh['rep'=32,'shard'=16] {'rep'}, use_global_device_ids=true, to_apply=%region_0.0 | all-reduce | flops 8192 | bytes 65536 | tf_op jit(solution)/shard_map/psum | solution.py:29
  235.2 0.2 fusion.12
  235.4 40.5 %psum.22 = f32[32,32]{0,1:T(8,128)S(1)} all-reduce(f32[32,32]{0,1:T(8,128)S(1)} %fusion.12), channel_id=1, replica_groups=mesh['rep'=32,'shard'=16] {'shard'}, use_global_device_ids=true, to_apply=%region_1.0 | all-reduce | flops 1024 | bytes 8192 | tf_op jit(solution)/shard_map/psum | solution.py:33
  275.9 0.1 copy.8
  276.0 2.9 cholesky.16
  278.9 0.6 compare_reduce_fusion
  279.6 0.7 fusion.7
  280.2 2.4 custom-call.7
  282.7 0.2 fusion.8
  282.9 1.7 fusion.13
  284.7 0.0 all-reduce.2.cloned.1.call-update
  284.7 468.0 %all-reduce.2.cloned.1.call-done = f32[1664,32]{0,1:T(8,128)} async-done(((f32[1664,32]{0,1:T(8,128)}), f32[1664,32]{0,1:T(8,128)}) %all-reduce.2.cloned.1.call-update) | async-done | bytes 213008 | tf_op jit(solution)/shard_map/psum | solution.py:42
  752.7 0.9 broadcast_multiply_fusion
  753.6 0.0 copy-start.1
  753.6 2.7 fusion.6
  756.3 0.0 copy-done.1
  (2 shorter events, 0.0 us)
Async XLA Ops:
  7.2 98.3 %copy-start = (bf16[1,2048,256]{2,1,0:T(8,128)(2,1)S(1)}, bf16[1,2048,256]{2,1,0:T(8,128)(2,1)}, u32[]{:S(2)}) copy-start(bf16[1,2048,256]{2,1,0:T(8,128)(2,1)} %param.4) | copy-start | bytes 3145732
  7.2 98.2 %all-gather.3.cloned.1.call-start = ((), (), s32[]{:S(2)}) async-start(), calls=%async_computation.1 | async-start | bytes 7241728 | tf_op jit(solution)/shard_map/all_gather | solution.py:24
  7.9 102.7 %copy-start.2 = (f32[1664,32]{0,1:T(8,128)S(1)}, f32[1664,32]{0,1:T(8,128)}, u32[]{:S(2)}) copy-start(f32[1664,32]{0,1:T(8,128)} %param.7) | copy-start | bytes 638980
  7.9 744.7 %all-reduce.2.cloned.1.call-start = ((), (), s32[]{:S(2)}) async-start(), calls=%async_computation | async-start | bytes 425984 | tf_op jit(solution)/shard_map/psum | solution.py:42
  753.6 2.7 copy-start.1
Sparse Core Ops, SparseCore 0:
  10.1 95.2 all-gather.2
  284.8 467.7 all-reduce.1
where the time goes:
time: 764 us; the launch traced here: 763 us
  waiting for transfers between devices  566 us (74%)
  blocking collectives  164 us (21%)
  between operations  14.1 us (2%)
  matrix products  11.6 us (2%)
    psum x1, waiting for transfers between devices, on_device(): right_factor = lax.psum(right_part, ('rep', 'shard')) / lax.axis_size('rep')  468 us
    psum x1, blocking collectives, on_device(): projected = lax.psum(partial_proj, 'rep')  123 us
    all_gather x1, waiting for transfers between devices, on_device(): lax.all_gather(local_grad, 'shard', axis=0, tiled=True)  97.5 us
    psum x1, blocking collectives, on_device(): gram_matrix = lax.psum(gram_part, 'shard')  40.5 us
  transfers between devices with their start and end apart: 2, of which 2 were waited for; matrix products, arithmetic and copies ran while one was open for 0% of the time, Pallas kernels for 0%

commit v1 on v0

v1 whole, which is shorter than its diff:
```python
import jax
import jax.numpy as jnp
from jax import lax
from jax.experimental import pallas as pl
from jax.experimental.pallas import tpu as pltpu
from jax.sharding import PartitionSpec as P

MESH = pl.DeviceIdType.MESH
F32, BF16 = jnp.float32, jnp.bfloat16
NZ, NR = 16, 32
TB, D, H, K = 128, 1664, 256, 32
PARTS = 2
ROWS = TB // PARTS
HELD = 5
P_OWNERS = 8
W_OWNERS = 26
NN = (((1,), (0,)), ((), ()))
NT = (((1,), (1,)), ((), ()))
TN = (((0,), (0,)), ((), ()))


def mm(a, b, dims):
    return lax.dot_general(a, b, dims, preferred_element_type=F32)


def split3(x):
    hi = x.astype(BF16)
    rest = x - hi.astype(F32)
    mid = rest.astype(BF16)
    low = (rest - mid.astype(F32)).astype(BF16)
    return hi, mid, low


def stack3(x):
    return jnp.concatenate(split3(x), axis=0)


def fold3(x):
    n = x.shape[0] // 3
    return x[:n] + (x[n : 2 * n] + x[2 * n :])


def columns(body):
    def step(i, carry):
        body(pl.ds(pl.multiple_of(i * 256, 256), 256))
        return carry

    lax.fori_loop(0, 6, step, 0)
    body(pl.ds(1536, 128))


def inverse_factor(packed):
    lane = lax.broadcasted_iota(jnp.int32, (8, 128), 1)
    sub = lax.broadcasted_iota(jnp.int32, (8, 128), 0)
    rows = []
    for q in range(4):
        g = pltpu.roll(packed, (32 - 32 * q) % 128, 1) if q != 1 else packed
        g = jnp.where((lane >= 32) & (lane < 64), g, 0.0)
        rows.append(g + jnp.where(lane == sub + 8 * q, 1.0, 0.0))
    for k in range(K):
        q, i = k // 8, k % 8
        row = rows[q][i : i + 1, :]
        pivot = row[:, 32 + k : 33 + k]
        inv = lax.rsqrt(pivot)
        inv = inv * (1.5 - 0.5 * pivot * inv * inv)
        row = row * inv
        for t in range(q, 4):
            col = rows[t][:, 32 + k : 33 + k] * inv
            new = rows[t] - col * row
            if t == q:
                new = jnp.where(sub > i, new, jnp.where(sub == i, row, rows[t]))
            rows[t] = new
    return jnp.concatenate(rows, axis=0)[:, 0:K]


def kernel(
    a_ref, b_ref, f_ref, r_ref, avg_ref, next_ref, rf_ref,
    ball, av, fv, rv, acc, br, psend, prs, ptot, gsend, grecv, ot,
    usend, urecv, wsend, wrs, wz, zrs, wfin,
    lsem, ssem, rsem, br_s, br_r, u_s, u_r, one_s, one_r,
):
    z = lax.axis_index("shard")
    me = lax.axis_index("rep")

    def zat(off):
        return lax.rem(z + (off + 2 * NZ), NZ)

    def block(owner):
        return pl.ds(pl.multiple_of(owner * TB, TB), TB)

    loads = [
        pltpu.make_async_copy(b_ref.at[0], ball.at[block(z)], lsem.at[0]),
        pltpu.make_async_copy(r_ref, rv, lsem.at[1]),
        pltpu.make_async_copy(f_ref.at[0], fv, lsem.at[2]),
        pltpu.make_async_copy(a_ref.at[0], av, lsem.at[3]),
    ]
    for load in loads:
        load.start()

    barrier = pltpu.get_barrier_semaphore()

    @pl.loop(1, NZ)
    def _(d):
        pl.semaphore_signal(barrier, inc=1, device_id={"shard": lax.rem(z + d, NZ)}, device_id_type=MESH)

    @pl.loop(1, NR)
    def _(d):
        pl.semaphore_signal(barrier, inc=1, device_id={"rep": lax.rem(me + d, NR)}, device_id_type=MESH)

    def wait_bytes(ref, sem):
        pltpu.make_async_copy(ref, ref, sem).wait()

    def piece(owner, part):
        return ball.at[pl.ds(pl.multiple_of(owner * TB + part * ROWS, ROWS), ROWS)]

    def ring(way, s, part):
        owner, to = (zat(-s), zat(1)) if way == 0 else (zat(s), zat(-1))
        return pltpu.make_async_remote_copy(
            piece(owner, part), piece(owner, part), ssem.at[way, s, part], rsem.at[way, s, part],
            device_id={"shard": to}, device_id_type=MESH,
        )

    def used(way, s, part):
        return s < 7 or (s == 7 and (part == 0) == (way == 0))

    def tick(k):
        s = k // PARTS
        for way in range(2):
            part = k % PARTS if way == 0 else PARTS - 1 - k % PARTS
            if used(way, s, part):
                ring(way, s, part).wait_recv()
                if used(way, s + 1, part):
                    ring(way, s + 1, part).start()

    def gather_terms(offsets):
        at = jnp.concatenate([av[block(zat(o)), :].T for o in offsets], axis=1)

        def body(cols):
            rows = jnp.concatenate([ball[block(zat(o)), cols] for o in offsets], axis=0)
            acc[:, cols] += mm(at, rows, NN)

        columns(body)

    loads[0].wait()
    loads[1].wait()
    r3 = stack3(rv[...])
    br[:, block(z)] = fold3(mm(r3, ball[block(z), :], NT))
    pl.semaphore_wait(barrier, NZ - 1 + NR - 1)

    for k in range(PARTS):
        for way in range(2):
            ring(way, 0, k if way == 0 else PARTS - 1 - k).start()

    def br_copy(d):
        return pltpu.make_async_remote_copy(
            br.at[:, block(z)], br.at[:, block(z)], br_s, br_r,
            device_id={"shard": lax.rem(z + d, NZ)}, device_id_type=MESH,
        )

    @pl.loop(1, NZ)
    def _(d):
        br_copy(d).start()

    loads[2].wait()
    fr = fold3(mm(r3, fv[...], NT))
    columns(lambda cols: acc.__setitem__((slice(None), cols), fv[:, cols].astype(F32)))
    loads[3].wait()
    wait_bytes(br.at[:, pl.ds(0, (NZ - 1) * TB)], br_r)
    psend[...] = fr + fold3(mm(stack3(br[...]), av[...], NN))

    def p_tile(o):
        return (
            pl.ds(pl.multiple_of(o // 2 * 8, 8), 8),
            pl.ds(pl.multiple_of(o % 2 * 128, 128), 128),
        )

    @pl.loop(0, P_OWNERS)
    def _(o):
        to = 4 * o

        @pl.when(to != me)
        def _():
            pltpu.make_async_remote_copy(
                psend.at[p_tile(o)], prs.at[lax.rem(me - to + (NR - 1), NR)], one_s.at[0], one_r.at[0],
                device_id={"rep": to}, device_id_type=MESH,
            ).start()

    tick(0)
    gather_terms([0])
    own_p = lax.rem(me, 4) == 0

    @pl.when(own_p)
    def _():
        wait_bytes(prs.at[pl.ds(0, NR - 1)], one_r.at[0])
        tile = p_tile(me // 4)
        ptot[tile] = jnp.sum(prs[0 : NR - 1], axis=0) + psend[tile]

        @pl.loop(1, NR)
        def _(d):
            pltpu.make_async_remote_copy(
                ptot.at[tile], ptot.at[tile], one_s.at[1], one_r.at[1],
                device_id={"rep": lax.rem(me + d, NR)}, device_id_type=MESH,
            ).start()

    tick(1)
    gather_terms([-1, 1])

    @pl.when(own_p)
    def _():
        wait_bytes(prs.at[pl.ds(0, P_OWNERS - 1)], one_r.at[1])

    @pl.when(jnp.logical_not(own_p))
    def _():
        wait_bytes(prs.at[pl.ds(0, P_OWNERS)], one_r.at[1])

    pt = ptot[...]
    p_hi, p_mid, p_low = split3(pt)
    wide = jnp.concatenate([pt] * 4, axis=0)
    w_hi, w_mid, w_low = split3(wide)
    g = mm(p_hi, w_hi, NT) + (
        (mm(p_hi, w_mid, NT) + mm(p_mid, w_hi, NT))
        + (mm(p_mid, w_mid, NT) + mm(p_hi, w_low, NT) + mm(p_low, w_hi, NT))
    )
    lane = lax.broadcasted_iota(jnp.int32, (8, 128), 1)
    packed = jnp.zeros((8, 128), F32)
    for q in range(4):
        packed = jnp.where((lane >= 32 * q) & (lane < 32 * q + 32), g[8 * q : 8 * q + 8], packed)
    gsend[...] = packed

    @pl.loop(1, NZ)
    def _(d):
        pltpu.make_async_remote_copy(
            gsend, grecv.at[d - 1], one_s.at[2], one_r.at[2],
            device_id={"shard": lax.rem(z + d, NZ)}, device_id_type=MESH,
        ).start()

    tick(2)
    wait_bytes(grecv.at[pl.ds(0, NZ - 1)], one_r.at[2])
    l_inv = inverse_factor(jnp.sum(grecv[0 : NZ - 1], axis=0) + gsend[...])
    tick(3)
    l_hi, l_mid, l_low = split3(l_inv)
    o_t = mm(l_hi, p_hi, NN) + (
        (mm(l_hi, p_mid, NN) + mm(l_mid, p_hi, NN))
        + (mm(l_mid, p_mid, NN) + mm(l_hi, p_low, NN) + mm(l_low, p_hi, NN))
    )
    ot[...] = o_t
    o3 = stack3(o_t)

    hops = [(o, o - HELD) for o in range(HELD + 1, 9)] + [(-o, HELD - o) for o in range(HELD + 1, 8)]

    def u_copy(i):
        return pltpu.make_async_remote_copy(
            usend.at[i], urecv.at[i], u_s.at[i], u_r.at[i],
            device_id={"shard": zat(hops[i][1])}, device_id_type=MESH,
        )

    for i, (o, _) in enumerate(hops):
        usend[i] = fold3(mm(o3, av[block(zat(o)), :], NT))
        u_copy(i).start()
    gather_terms([-2, 2])
    for s in range(3, HELD + 1):
        tick(2 * s - 2)
        tick(2 * s - 1)
        gather_terms([-s, s])
    for i in range(len(hops)):
        u_copy(i).wait_recv()
    u_up = sum(urecv[i] for i in range(len(hops)) if hops[i][0] > 0)
    u_down = sum(urecv[i] for i in range(len(hops)) if hops[i][0] < 0)
    u3 = stack3(jnp.concatenate([u_up, u_down], axis=1))

    def w_terms(cols):
        m_hi, m_mid, _ = split3(acc[:, cols])
        rows = jnp.concatenate([ball[block(zat(HELD)), cols], ball[block(zat(-HELD)), cols]], axis=0)
        total = mm(o3, m_hi, NN) + mm(u3, rows, NN)
        cross = mm(o3[: 2 * K], m_mid, NN)
        wsend[:, cols] = fold3(total) + (cross[:K] + cross[K:])

    columns(w_terms)

    def w_chunk(q):
        return (
            pl.ds(pl.multiple_of(lax.rem(q, 2) * 16, 16), 16),
            pl.ds(pl.multiple_of(q // 2 * 128, 128), 128),
        )

    @pl.loop(0, W_OWNERS)
    def _(q):
        @pl.when(q != me)
        def _():
            pltpu.make_async_remote_copy(
                wsend.at[w_chunk(q)], wrs.at[lax.rem(me - q + (NR - 1), NR)], one_s.at[3], one_r.at[3],
                device_id={"rep": q}, device_id_type=MESH,
            ).start()

    tick(2 * HELD)
    own_w = me < W_OWNERS
    base = lax.rem(me, 8)
    which = z // 8
    own_z = own_w & (lax.rem(z, 8) == base)
    z_tile = pl.ds(pl.multiple_of(which * 8, 8), 8)

    @pl.when(own_w)
    def _():
        wait_bytes(wrs.at[pl.ds(0, NR - 1)], one_r.at[3])
        wz[...] = jnp.sum(wrs[0 : NR - 1], axis=0) + wsend[w_chunk(me)]
        for i in range(2):
            to = base + 8 * i

            @pl.when(to != z)
            def _():
                pltpu.make_async_remote_copy(
                    wz.at[pl.ds(8 * i, 8)], zrs.at[lax.rem(z - to + (NZ - 1), NZ)], one_s.at[4 + i], one_r.at[4],
                    device_id={"shard": to}, device_id_type=MESH,
                ).start()

    tick(2 * HELD + 1)
    gather_terms([-(HELD + 1), HELD + 1])

    @pl.when(own_z)
    def _():
        wait_bytes(zrs.at[pl.ds(0, NZ - 1)], one_r.at[4])
        wfin[z_tile, :] = (jnp.sum(zrs[0 : NZ - 1], axis=0) + wz[z_tile, :]) * (1.0 / NR)

        @pl.loop(1, NZ)
        def _(d):
            pltpu.make_async_remote_copy(
                wfin.at[z_tile], wfin.at[z_tile], one_s.at[6], one_r.at[5 + which],
                device_id={"shard": lax.rem(z + d, NZ)}, device_id_type=MESH,
            ).start()

    tick(2 * HELD + 2)

    @pl.when(own_w)
    def _():
        for i in range(2):
            @pl.when(base + 8 * i != z)
            def _():
                wait_bytes(wfin.at[pl.ds(8 * i, 8)], one_r.at[5 + i])

        rf_ref[w_chunk(me)] = wfin[...]

        @pl.loop(1, NR)
        def _(d):
            pltpu.make_async_remote_copy(
                wfin, rf_ref.at[w_chunk(me)], one_s.at[7], one_r.at[7],
                device_id={"rep": lax.rem(me + d, NR)}, device_id_type=MESH,
            ).start()

    tick(2 * HELD + 3)
    gather_terms([-(HELD + 2), HELD + 2])

    @pl.when(own_w)
    def _():
        wait_bytes(wrs.at[pl.ds(0, W_OWNERS - 1)], one_r.at[7])

    @pl.when(jnp.logical_not(own_w))
    def _():
        wait_bytes(wrs.at[pl.ds(0, W_OWNERS)], one_r.at[7])

    o_hi, o_mid, o_low = split3(ot[...])
    lhs = jnp.concatenate([o_hi, o_hi, o_mid, o_mid, o_hi, o_low], axis=0)

    def rebuild(cols):
        h, m, low = split3(rf_ref[:, cols])
        rebuilt = mm(lhs, jnp.concatenate([h, m, h, m, low, h], axis=0), TN)
        avg_ref[:, cols] = rebuilt.astype(BF16)
        acc[:, cols] -= rebuilt

    columns(rebuild)
    tick(14)
    tick(15)
    last = av[block(zat(8)), :].T

    def finish(cols):
        next_ref[0, :, cols] = (acc[:, cols] + mm(last, ball[block(zat(8)), cols], NN)).astype(BF16)

    columns(finish)

    for k in range(8 * PARTS):
        for way in range(2):
            if used(way, k // PARTS, k % PARTS):
                ring(way, k // PARTS, k % PARTS).wait_send()
    wait_bytes(br.at[:, pl.ds(0, (NZ - 1) * TB)], br_s)
    for i in range(len(hops)):
        u_copy(i).wait_send()
    wait_bytes(grecv.at[pl.ds(0, NZ - 1)], one_s.at[2])

    @pl.when(own_p)
    def _():
        wait_bytes(prs.at[pl.ds(0, P_OWNERS - 1)], one_s.at[0])
        wait_bytes(prs.at[pl.ds(0, NR - 1)], one_s.at[1])

    @pl.when(jnp.logical_not(own_p))
    def _():
        wait_bytes(prs.at[pl.ds(0, P_OWNERS)], one_s.at[0])

    @pl.when(own_w)
    def _():
        wait_bytes(wrs.at[pl.ds(0, W_OWNERS - 1)], one_s.at[3])
        for i in range(2):
            @pl.when(base + 8 * i != z)
            def _():
                wait_bytes(wz.at[pl.ds(8 * i, 8)], one_s.at[4 + i])

        wait_bytes(wrs.at[pl.ds(0, NR - 1)], one_s.at[7])

    @pl.when(jnp.logical_not(own_w))
    def _():
        wait_bytes(wrs.at[pl.ds(0, W_OWNERS)], one_s.at[3])

    @pl.when(own_z)
    def _():
        wait_bytes(zrs.at[pl.ds(0, NZ - 1)], one_s.at[6])


def on_device(activations, output_grad, feedback, right_start):
    n_hops = (8 - HELD) + (7 - HELD)
    dma = pltpu.SemaphoreType.DMA
    averaged, feedback_next, right_t = pl.pallas_call(
        kernel,
        out_shape=(
            jax.ShapeDtypeStruct((H, D), BF16),
            jax.ShapeDtypeStruct((1, H, D), BF16),
            jax.ShapeDtypeStruct((K, D), F32),
        ),
        in_specs=[pl.BlockSpec(memory_space=pltpu.HBM)] * 4,
        out_specs=[pl.BlockSpec(memory_space=pltpu.VMEM)] * 3,
        scratch_shapes=[
            pltpu.VMEM((NZ * TB, D), BF16),
            pltpu.VMEM((NZ * TB, H), BF16),
            pltpu.VMEM((H, D), BF16),
            pltpu.VMEM((K, D), F32),
            pltpu.VMEM((H, D), F32),
            pltpu.VMEM((K, NZ * TB), F32),
            pltpu.VMEM((K, H), F32),
            pltpu.VMEM((NR, 8, 128), F32),
            pltpu.VMEM((K, H), F32),
            pltpu.VMEM((8, 128), F32),
            pltpu.VMEM((NZ, 8, 128), F32),
            pltpu.VMEM((K, H), F32),
            pltpu.VMEM((n_hops, K, TB), F32),
            pltpu.VMEM((n_hops, K, TB), F32),
            pltpu.VMEM((K, D), F32),
            pltpu.VMEM((NR, 16, 128), F32),
            pltpu.VMEM((16, 128), F32),
            pltpu.VMEM((NZ, 8, 128), F32),
            pltpu.VMEM((16, 128), F32),
            dma((4,)),
            dma((2, 8, PARTS)),
            dma((2, 8, PARTS)),
            dma,
            dma,
            dma((n_hops,)),
            dma((n_hops,)),
            dma((8,)),
            dma((8,)),
        ],
        compiler_params=pltpu.CompilerParams(
            collective_id=0, has_side_effects=True, vmem_limit_bytes=48 * 2**20
        ),
        cost_estimate=pl.CostEstimate(
            flops=2 * H * NZ * TB * D, bytes_accessed=5_000_000, transcendentals=0
        ),
    )(activations, output_grad, feedback, right_start.T)
    return averaged, feedback_next, right_t.T


def solution(mesh):
    return jax.shard_map(
        on_device,
        mesh=mesh,
        in_specs=(P("rep", None, "shard"), P("rep", "shard", None), P("rep", "shard", None), P()),
        out_specs=(P("shard", None), P("rep", "shard", None), P()),
        check_vma=False,
    )
```

time: 764 us -> 135 us (0.18)
  waiting for transfers between devices: 566 us -> 0 us
  blocking collectives: 164 us -> 0 us
  Pallas kernels: 0 us -> 127 us
  between operations: 14.1 us -> 0.65 us
  matrix products: 11.6 us -> 0 us
    psum x1 -> x0, waiting for transfers between devices: 468 us -> none  [on_device(): right_factor = lax.psum(right_part, ('rep', 'shard')) / lax.axis_size('rep')]
    psum x2 -> x0, blocking collectives: 164 us -> none  [the longest x1 123 us: on_device(): projected = lax.psum(partial_proj, 'rep')]
    pallas_call x0 -> x1, Pallas kernels: none -> 127 us  [on_device(): pl.pallas_call(kernel, out_shape=(jax.ShapeDtypeStruct((H, D), BF16), jax...]
    all_gather x1 -> x0, waiting for transfers between devices: 97.5 us -> none  [on_device(): lax.all_gather(local_grad, 'shard', axis=0, tiled=True)]
    dot_general x5 -> x0, matrix products: 11.3 us -> none  [the longest x1 5.18 us: add_outer(): lax.dot_general(activations_local, piece, (((0,), (0,)), ((), ())), prefe...]
  transfers between devices with their start and end apart: 2 -> 0, of which waited for: 2 -> 0; matrix products, arithmetic and copies ran while one was open for 0% -> 0% of each run, Pallas kernels for 0% -> 0%
where the time goes in v1:
time: 135 us
  Pallas kernels  127 us (94%)
  local copies, waits for them, and re-layouts  6.8 us (5%)
    pallas_call x1, Pallas kernels, on_device(): pl.pallas_call(kernel, out_shape=(jax.ShapeDtypeStruct((H, D), BF16), jax...  127 us
    unnamed x11, local copies, waits for them, and re-layouts  6.8 us

profile of v1, /device:TPU:1, one launch (start us, length us, event | category | flops | bytes accessed | tf_op | source)
XLA Modules:
  0.0 134.9 jit_solution(1140017260233532523)
XLA Ops:
  0.6 0.0 copy-start
  0.6 1.2 copy-done
  1.9 0.0 copy-start.1
  1.9 1.2 copy-done.1
  3.0 0.0 copy-start.2
  3.0 1.0 copy-done.2
  4.0 0.0 copy-start.3
  4.0 0.9 copy-done.3
  5.0 127.4 %shard_map.67 = (bf16[256,1664]{1,0:T(8,128)(2,1)S(1)}, bf16[1,256,1664]{2,1,0:T(8,128)(2,1)S(1)}, f32[32,1664]{1,0:T(8,128)S(1)}) custom-call(bf16[1,2048,256]{2,1,0:T(8,128)(2,1)S(1)} %copy-done, bf16[1,128,1664]{2,1,0:T(8,128)(2,1)S(1)} %copy-done.2, bf16[1,256,1664]{2,1,0:T(8,128)(2,1)S(1)} %copy-done.1, f32[32,1664]{1,0:T(8,128)S(1)} %bitcast.3), custom_call_target="tpu_custom_call" | custom-call | flops 1744830464 | bytes 5000000 | tf_op jit(solution)/shard_map/pallas_call | solution.py:419
  132.4 0.9 copy.10
  133.3 0.9 copy.11
  134.2 0.7 copy.12
Async XLA Ops:
  0.6 1.2 copy-start
  1.9 1.2 copy-start.1
  3.0 1.0 copy-start.2
  4.0 0.9 copy-start.3

commit v2 on v1

--- a/solution.py
+++ b/solution.py
@@ -9,11 +9,12 @@
 F32, BF16 = jnp.float32, jnp.bfloat16
 NZ, NR = 16, 32
 TB, D, H, K = 128, 1664, 256, 32
-PARTS = 2
+PARTS = 4
 ROWS = TB // PARTS
-HELD = 5
+HELD = 4
 P_OWNERS = 8
 W_OWNERS = 26
+AT = (0, 2, 3, 5, 7, 9, 10, 12, 13, 17, 20, 22, 24, 25, 26)
 NN = (((1,), (0,)), ((), ()))
 NT = (((1,), (1,)), ((), ()))
 TN = (((0,), (0,)), ((), ()))
@@ -75,9 +76,9 @@
 
 def kernel(
     a_ref, b_ref, f_ref, r_ref, avg_ref, next_ref, rf_ref,
-    ball, av, fv, rv, acc, br, psend, prs, ptot, gsend, grecv, ot,
-    usend, urecv, wsend, wrs, wz, zrs, wfin,
-    lsem, ssem, rsem, br_s, br_r, u_s, u_r, one_s, one_r,
+    ball, av, fv, rv, acc, br, psend, prs, ptot, gsum, ot,
+    usend, urecv, wsend, wrs, wsum,
+    lsem, ssem, rsem, u_s, u_r, one_s, one_r,
 ):
     z = lax.axis_index("shard")
     me = lax.axis_index("rep")
@@ -115,22 +116,27 @@
 
     def ring(way, s, part):
         owner, to = (zat(-s), zat(1)) if way == 0 else (zat(s), zat(-1))
+        source = piece(owner, part) if s else b_ref.at[0, pl.ds(part * ROWS, ROWS)]
         return pltpu.make_async_remote_copy(
-            piece(owner, part), piece(owner, part), ssem.at[way, s, part], rsem.at[way, s, part],
+            source, piece(owner, part), ssem.at[way, s, part], rsem.at[way, s, part],
             device_id={"shard": to}, device_id_type=MESH,
         )
 
     def used(way, s, part):
-        return s < 7 or (s == 7 and (part == 0) == (way == 0))
-
-    def tick(k):
-        s = k // PARTS
-        for way in range(2):
-            part = k % PARTS if way == 0 else PARTS - 1 - k % PARTS
-            if used(way, s, part):
-                ring(way, s, part).wait_recv()
-                if used(way, s + 1, part):
-                    ring(way, s + 1, part).start()
+        return s < 7 or (s == 7 and (part < PARTS // 2) == (way == 0))
+
+    done = [0]
+
+    def ticks(upto):
+        for k in range(done[0], upto):
+            s = k // PARTS
+            for way in range(2):
+                part = k % PARTS if way == 0 else PARTS - 1 - k % PARTS
+                if used(way, s, part):
+                    ring(way, s, part).wait_recv()
+                    if used(way, s + 1, part):
+                        ring(way, s + 1, part).start()
+        done[0] = max(done[0], upto)
 
     def gather_terms(offsets):
         at = jnp.concatenate([av[block(zat(o)), :].T for o in offsets], axis=1)
@@ -141,32 +147,62 @@
 
         columns(body)
 
+    pl.semaphore_wait(barrier, NZ - 1 + NR - 1)
+    for k in range(PARTS):
+        for way in range(2):
+            ring(way, 0, k if way == 0 else PARTS - 1 - k).start()
+
     loads[0].wait()
     loads[1].wait()
     r3 = stack3(rv[...])
-    br[:, block(z)] = fold3(mm(r3, ball[block(z), :], NT))
-    pl.semaphore_wait(barrier, NZ - 1 + NR - 1)
-
-    for k in range(PARTS):
-        for way in range(2):
-            ring(way, 0, k if way == 0 else PARTS - 1 - k).start()
-
-    def br_copy(d):
-        return pltpu.make_async_remote_copy(
-            br.at[:, block(z)], br.at[:, block(z)], br_s, br_r,
-            device_id={"shard": lax.rem(z + d, NZ)}, device_id_type=MESH,
-        )
-
-    @pl.loop(1, NZ)
-    def _(d):
-        br_copy(d).start()
+    br[z] = fold3(mm(r3, ball[block(z), :], NT))
+
+    def br_send(owner, off, i):
+        pltpu.make_async_remote_copy(
+            br.at[owner], br.at[owner], one_s.at[i], one_r.at[i],
+            device_id={"shard": zat(off)}, device_id_type=MESH,
+        ).start()
+
+    for off in (6, -6, 3, -3):
+        br_send(z, off, 8)
+    for off in (1, -1):
+        br_send(z, off, 9)
 
     loads[2].wait()
     fr = fold3(mm(r3, fv[...], NT))
     columns(lambda cols: acc.__setitem__((slice(None), cols), fv[:, cols].astype(F32)))
     loads[3].wait()
-    wait_bytes(br.at[:, pl.ds(0, (NZ - 1) * TB)], br_r)
-    psend[...] = fr + fold3(mm(stack3(br[...]), av[...], NN))
+    ticks(AT[0])
+    wait_bytes(br.at[pl.ds(0, 4)], one_r.at[8])
+    for off in (1, -1):
+        for o in (3, -3, 6, -6):
+            br_send(zat(o), off, 9)
+    br_send(zat(-6), 2, 9)
+    ticks(AT[1])
+    wait_bytes(br.at[pl.ds(0, 11)], one_r.at[9])
+    br3 = stack3(jnp.concatenate([br[i] for i in range(NZ)], axis=1))
+    psend[...] = fr + fold3(mm(br3, av[...], NN))
+
+    def z_first(ref, i):
+        for off in (4, 8, 12):
+            pltpu.make_async_remote_copy(
+                ref.at[z // 4], ref.at[z // 4], one_s.at[i], one_r.at[i],
+                device_id={"shard": zat(off)}, device_id_type=MESH,
+            ).start()
+
+    def z_second(ref, i):
+        wait_bytes(ref.at[pl.ds(0, 3)], one_r.at[i])
+        mine = 4 + lax.rem(z, 4)
+        ref[mine] = (ref[0] + ref[1]) + (ref[2] + ref[3])
+        for off in (1, 2, -1):
+            pltpu.make_async_remote_copy(
+                ref.at[mine], ref.at[mine], one_s.at[i + 1], one_r.at[i + 1],
+                device_id={"shard": zat(off)}, device_id_type=MESH,
+            ).start()
+
+    def z_total(ref, i):
+        wait_bytes(ref.at[pl.ds(0, 3)], one_r.at[i + 1])
+        return (ref[4] + ref[5]) + (ref[6] + ref[7])
 
     def p_tile(o):
         return (
@@ -185,8 +221,9 @@
                 device_id={"rep": to}, device_id_type=MESH,
             ).start()
 
-    tick(0)
+    ticks(AT[2])
     gather_terms([0])
+    ticks(AT[3])
     own_p = lax.rem(me, 4) == 0
 
     @pl.when(own_p)
@@ -202,8 +239,8 @@
                 device_id={"rep": lax.rem(me + d, NR)}, device_id_type=MESH,
             ).start()
 
-    tick(1)
     gather_terms([-1, 1])
+    ticks(AT[4])
 
     @pl.when(own_p)
     def _():
@@ -225,19 +262,15 @@
     packed = jnp.zeros((8, 128), F32)
     for q in range(4):
         packed = jnp.where((lane >= 32 * q) & (lane < 32 * q + 32), g[8 * q : 8 * q + 8], packed)
-    gsend[...] = packed
-
-    @pl.loop(1, NZ)
-    def _(d):
-        pltpu.make_async_remote_copy(
-            gsend, grecv.at[d - 1], one_s.at[2], one_r.at[2],
-            device_id={"shard": lax.rem(z + d, NZ)}, device_id_type=MESH,
-        ).start()
-
-    tick(2)
-    wait_bytes(grecv.at[pl.ds(0, NZ - 1)], one_r.at[2])
-    l_inv = inverse_factor(jnp.sum(grecv[0 : NZ - 1], axis=0) + gsend[...])
-    tick(3)
+    gsum[z // 4] = packed
+    z_first(gsum, 2)
+    ticks(AT[5])
+    gather_terms([-2, 2])
+    ticks(AT[6])
+    z_second(gsum, 2)
+    ticks(AT[7])
+    l_inv = inverse_factor(z_total(gsum, 2))
+    ticks(AT[8])
     l_hi, l_mid, l_low = split3(l_inv)
     o_t = mm(l_hi, p_hi, NN) + (
         (mm(l_hi, p_mid, NN) + mm(l_mid, p_hi, NN))
@@ -257,10 +290,8 @@
     for i, (o, _) in enumerate(hops):
         usend[i] = fold3(mm(o3, av[block(zat(o)), :], NT))
         u_copy(i).start()
-    gather_terms([-2, 2])
     for s in range(3, HELD + 1):
-        tick(2 * s - 2)
-        tick(2 * s - 1)
+        ticks(PARTS * s)
         gather_terms([-s, s])
     for i in range(len(hops)):
         u_copy(i).wait_recv()
@@ -288,66 +319,43 @@
         @pl.when(q != me)
         def _():
             pltpu.make_async_remote_copy(
-                wsend.at[w_chunk(q)], wrs.at[lax.rem(me - q + (NR - 1), NR)], one_s.at[3], one_r.at[3],
+                wsend.at[w_chunk(q)], wrs.at[lax.rem(me - q + (NR - 1), NR)], one_s.at[4], one_r.at[4],
                 device_id={"rep": q}, device_id_type=MESH,
             ).start()
 
-    tick(2 * HELD)
+    ticks(AT[9])
     own_w = me < W_OWNERS
-    base = lax.rem(me, 8)
-    which = z // 8
-    own_z = own_w & (lax.rem(z, 8) == base)
-    z_tile = pl.ds(pl.multiple_of(which * 8, 8), 8)
 
     @pl.when(own_w)
     def _():
-        wait_bytes(wrs.at[pl.ds(0, NR - 1)], one_r.at[3])
-        wz[...] = jnp.sum(wrs[0 : NR - 1], axis=0) + wsend[w_chunk(me)]
-        for i in range(2):
-            to = base + 8 * i
-
-            @pl.when(to != z)
-            def _():
-                pltpu.make_async_remote_copy(
-                    wz.at[pl.ds(8 * i, 8)], zrs.at[lax.rem(z - to + (NZ - 1), NZ)], one_s.at[4 + i], one_r.at[4],
-                    device_id={"shard": to}, device_id_type=MESH,
-                ).start()
-
-    tick(2 * HELD + 1)
-    gather_terms([-(HELD + 1), HELD + 1])
-
-    @pl.when(own_z)
-    def _():
-        wait_bytes(zrs.at[pl.ds(0, NZ - 1)], one_r.at[4])
-        wfin[z_tile, :] = (jnp.sum(zrs[0 : NZ - 1], axis=0) + wz[z_tile, :]) * (1.0 / NR)
-
-        @pl.loop(1, NZ)
-        def _(d):
-            pltpu.make_async_remote_copy(
-                wfin.at[z_tile], wfin.at[z_tile], one_s.at[6], one_r.at[5 + which],
-                device_id={"shard": lax.rem(z + d, NZ)}, device_id_type=MESH,
-            ).start()
-
-    tick(2 * HELD + 2)
+        wait_bytes(wrs.at[pl.ds(0, NR - 1)], one_r.at[4])
+        wsum[z // 4] = jnp.sum(wrs[0 : NR - 1], axis=0) + wsend[w_chunk(me)]
+        z_first(wsum, 5)
+
+    ticks(AT[10])
+    gather_terms([-5, 5])
+    ticks(AT[11])
 
     @pl.when(own_w)
     def _():
-        for i in range(2):
-            @pl.when(base + 8 * i != z)
-            def _():
-                wait_bytes(wfin.at[pl.ds(8 * i, 8)], one_r.at[5 + i])
-
-        rf_ref[w_chunk(me)] = wfin[...]
+        z_second(wsum, 5)
+
+    ticks(AT[12])
+
+    @pl.when(own_w)
+    def _():
+        rf_ref[w_chunk(me)] = z_total(wsum, 5) * (1.0 / NR)
 
         @pl.loop(1, NR)
         def _(d):
             pltpu.make_async_remote_copy(
-                wfin, rf_ref.at[w_chunk(me)], one_s.at[7], one_r.at[7],
+                rf_ref.at[w_chunk(me)], rf_ref.at[w_chunk(me)], one_s.at[7], one_r.at[7],
                 device_id={"rep": lax.rem(me + d, NR)}, device_id_type=MESH,
             ).start()
 
-    tick(2 * HELD + 3)
-    gather_terms([-(HELD + 2), HELD + 2])
+    ticks(AT[13])
+    gather_terms([-6, 6])
+    ticks(AT[14])
 
     @pl.when(own_w)
     def _():
@@ -367,8 +375,9 @@
         acc[:, cols] -= rebuilt
 
     columns(rebuild)
-    tick(14)
-    tick(15)
+    ticks(PARTS * 7)
+    gather_terms([-7, 7])
+    ticks(PARTS * 8)
     last = av[block(zat(8)), :].T
 
     def finish(cols):
@@ -380,10 +389,12 @@
         for way in range(2):
             if used(way, k // PARTS, k % PARTS):
                 ring(way, k // PARTS, k % PARTS).wait_send()
-    wait_bytes(br.at[:, pl.ds(0, (NZ - 1) * TB)], br_s)
+    wait_bytes(br.at[pl.ds(0, 4)], one_s.at[8])
+    wait_bytes(br.at[pl.ds(0, 11)], one_s.at[9])
     for i in range(len(hops)):
         u_copy(i).wait_send()
-    wait_bytes(grecv.at[pl.ds(0, NZ - 1)], one_s.at[2])
+    for i in (2, 3):
+        wait_bytes(gsum.at[pl.ds(0, 3)], one_s.at[i])
 
     @pl.when(own_p)
     def _():
@@ -396,33 +407,39 @@
 
     @pl.when(own_w)
     def _():
-        wait_bytes(wrs.at[pl.ds(0, W_OWNERS - 1)], one_s.at[3])
-        for i in range(2):
-            @pl.when(base + 8 * i != z)
-            def _():
-                wait_bytes(wz.at[pl.ds(8 * i, 8)], one_s.at[4 + i])
-
+        wait_bytes(wrs.at[pl.ds(0, W_OWNERS - 1)], one_s.at[4])
+        for i in (5, 6):
+            wait_bytes(wsum.at[pl.ds(0, 3)], one_s.at[i])
         wait_bytes(wrs.at[pl.ds(0, NR - 1)], one_s.at[7])
 
     @pl.when(jnp.logical_not(own_w))
     def _():
-        wait_bytes(wrs.at[pl.ds(0, W_OWNERS)], one_s.at[3])
-
-    @pl.when(own_z)
-    def _():
-        wait_bytes(zrs.at[pl.ds(0, NZ - 1)], one_s.at[6])
+        wait_bytes(wrs.at[pl.ds(0, W_OWNERS)], one_s.at[4])
+
+
+def store(avg_ref, next_ref, rf_ref, avg_out, next_out, rf_out, sem):
+    copies = [
+        pltpu.make_async_copy(avg_ref, avg_out, sem.at[0]),
+        pltpu.make_async_copy(next_ref, next_out, sem.at[1]),
+        pltpu.make_async_copy(rf_ref, rf_out, sem.at[2]),
+    ]
+    for copy in copies:
+        copy.start()
+    for copy in copies:
+        copy.wait()
 
 
 def on_device(activations, output_grad, feedback, right_start):
     n_hops = (8 - HELD) + (7 - HELD)
     dma = pltpu.SemaphoreType.DMA
-    averaged, feedback_next, right_t = pl.pallas_call(
+    shapes = (
+        jax.ShapeDtypeStruct((H, D), BF16),
+        jax.ShapeDtypeStruct((1, H, D), BF16),
+        jax.ShapeDtypeStruct((K, D), F32),
+    )
+    results = pl.pallas_call(
         kernel,
-        out_shape=(
-            jax.ShapeDtypeStruct((H, D), BF16),
-            jax.ShapeDtypeStruct((1, H, D), BF16),
-            jax.ShapeDtypeStruct((K, D), F32),
-        ),
+        out_shape=tuple(pltpu.VMEM(s.shape, s.dtype) for s in shapes),
         in_specs=[pl.BlockSpec(memory_space=pltpu.HBM)] * 4,
         out_specs=[pl.BlockSpec(memory_space=pltpu.VMEM)] * 3,
         scratch_shapes=[
@@ -431,37 +448,40 @@
             pltpu.VMEM((H, D), BF16),
             pltpu.VMEM((K, D), F32),
             pltpu.VMEM((H, D), F32),
-            pltpu.VMEM((K, NZ * TB), F32),
+            pltpu.VMEM((NZ, K, TB), F32),
             pltpu.VMEM((K, H), F32),
             pltpu.VMEM((NR, 8, 128), F32),
             pltpu.VMEM((K, H), F32),
-            pltpu.VMEM((8, 128), F32),
-            pltpu.VMEM((NZ, 8, 128), F32),
+            pltpu.VMEM((8, 8, 128), F32),
             pltpu.VMEM((K, H), F32),
             pltpu.VMEM((n_hops, K, TB), F32),
             pltpu.VMEM((n_hops, K, TB), F32),
             pltpu.VMEM((K, D), F32),
             pltpu.VMEM((NR, 16, 128), F32),
-            pltpu.VMEM((16, 128), F32),
-            pltpu.VMEM((NZ, 8, 128), F32),
-            pltpu.VMEM((16, 128), F32),
+            pltpu.VMEM((8, 16, 128), F32),
             dma((4,)),
             dma((2, 8, PARTS)),
             dma((2, 8, PARTS)),
-            dma,
-            dma,
             dma((n_hops,)),
             dma((n_hops,)),
-            dma((8,)),
-            dma((8,)),
+            dma((10,)),
+            dma((10,)),
         ],
         compiler_params=pltpu.CompilerParams(
-            collective_id=0, has_side_effects=True, vmem_limit_bytes=48 * 2**20
+            collective_id=0, has_side_effects=True, vmem_limit_bytes=61 * 2**20
         ),
         cost_estimate=pl.CostEstimate(
             flops=2 * H * NZ * TB * D, bytes_accessed=5_000_000, transcendentals=0
         ),
     )(activations, output_grad, feedback, right_start.T)
+    averaged, feedback_next, right_t = pl.pallas_call(
+        store,
+        out_shape=shapes,
+        in_specs=[pl.BlockSpec(memory_space=pl.ANY)] * 3,
+        out_specs=[pl.BlockSpec(memory_space=pltpu.HBM)] * 3,
+        scratch_shapes=[dma((3,))],
+        compiler_params=pltpu.CompilerParams(vmem_limit_bytes=2**20),
+    )(*results)
     return averaged, feedback_next, right_t.T
 
 

time: 135 us -> 110 us (0.81)
  Pallas kernels: 127 us -> 109 us
  local copies, waits for them, and re-layouts: 6.8 us -> 0 us
    pallas_call x1 -> x2, Pallas kernels: 127 us -> 109 us  [the longest x1 108 us: on_device(): pl.pallas_call(kernel, out_shape=tuple((pltpu.VMEM(s.shape, s.dtype) for...]
    unnamed x11 -> x0, local copies, waits for them, and re-layouts: 6.8 us -> none
where the time goes in v2:
time: 110 us
  Pallas kernels  109 us (99%)
    pallas_call x1, Pallas kernels, on_device(): pl.pallas_call(kernel, out_shape=tuple((pltpu.VMEM(s.shape, s.dtype) for...  108 us

profile of v2, /device:TPU:1, one launch (start us, length us, event | category | flops | bytes accessed | tf_op | source)
XLA Modules:
  0.0 109.7 jit_solution(1911797470814519627)
XLA Ops:
  0.6 107.7 %shard_map.67 = (bf16[256,1664]{1,0:T(8,128)(2,1)S(1)}, bf16[1,256,1664]{2,1,0:T(8,128)(2,1)S(1)}, f32[32,1664]{1,0:T(8,128)S(1)}) custom-call(bf16[1,2048,256]{2,1,0:T(8,128)(2,1)} %a_ref.1, bf16[1,128,1664]{2,1,0:T(8,128)(2,1)} %b_ref.1, bf16[1,256,1664]{2,1,0:T(8,128)(2,1)} %f_ref.1, f32[32,1664]{1,0:T(8,128)} %bitcast.2), custom_call_target="tpu_custom_call" | custom-call | flops 1744830464 | bytes 5000000 | tf_op jit(solution)/shard_map/pallas_call | solution.py:440
  108.4 1.3 %shard_map.68 = (bf16[256,1664]{1,0:T(8,128)(2,1)}, bf16[1,256,1664]{2,1,0:T(8,128)(2,1)}, f32[32,1664]{1,0:T(8,128)}) custom-call(bf16[256,1664]{1,0:T(8,128)(2,1)S(1)} %get-tuple-element.9.avg_ref, bf16[1,256,1664]{2,1,0:T(8,128)(2,1)S(1)} %get-tuple-element.10.next_ref, f32[32,1664]{1,0:T(8,128)S(1)} %get-tuple-element.11.rf_ref), custom_call_target="tpu_custom_call" | custom-call | tf_op jit(solution)/shard_map/pallas_call | solution.py:477

commit v3 on v2

--- a/solution.py
+++ b/solution.py
@@ -12,9 +12,10 @@
 PARTS = 4
 ROWS = TB // PARTS
 HELD = 4
+NEAR = (3, -3, 2, -2, 1, -1)
 P_OWNERS = 8
 W_OWNERS = 26
-AT = (0, 2, 3, 5, 7, 9, 10, 12, 13, 17, 20, 22, 24, 25, 26)
+AT = (1, 2, 4, 6, 8, 11, 14, 16, 22, 25, 27, 30, 32)
 NN = (((1,), (0,)), ((), ()))
 NT = (((1,), (1,)), ((), ()))
 TN = (((0,), (0,)), ((), ()))
@@ -100,9 +101,8 @@
 
     barrier = pltpu.get_barrier_semaphore()
 
-    @pl.loop(1, NZ)
-    def _(d):
-        pl.semaphore_signal(barrier, inc=1, device_id={"shard": lax.rem(z + d, NZ)}, device_id_type=MESH)
+    for off in NEAR:
+        pl.semaphore_signal(barrier, inc=1, device_id={"shard": zat(off)}, device_id_type=MESH)
 
     @pl.loop(1, NR)
     def _(d):
@@ -128,9 +128,12 @@
     done = [0]
 
     def ticks(upto):
-        for k in range(done[0], upto):
+        for k in range(done[0] - PARTS, upto - PARTS):
             s = k // PARTS
             for way in range(2):
+                if s < 0:
+                    ring(way, 0, k + PARTS if way == 0 else -1 - k).start()
+                    continue
                 part = k % PARTS if way == 0 else PARTS - 1 - k % PARTS
                 if used(way, s, part):
                     ring(way, s, part).wait_recv()
@@ -139,6 +142,7 @@
         done[0] = max(done[0], upto)
 
     def gather_terms(offsets):
+        ticks(PARTS * (max(offsets) + 1) if max(offsets) else 0)
         at = jnp.concatenate([av[block(zat(o)), :].T for o in offsets], axis=1)
 
         def body(cols):
@@ -147,10 +151,8 @@
 
         columns(body)
 
-    pl.semaphore_wait(barrier, NZ - 1 + NR - 1)
-    for k in range(PARTS):
-        for way in range(2):
-            ring(way, 0, k if way == 0 else PARTS - 1 - k).start()
+    pl.semaphore_wait(barrier, len(NEAR) + NR - 1)
+    ticks(AT[0])
 
     loads[0].wait()
     loads[1].wait()
@@ -163,7 +165,7 @@
             device_id={"shard": zat(off)}, device_id_type=MESH,
         ).start()
 
-    for off in (6, -6, 3, -3):
+    for off in (3, -3):
         br_send(z, off, 8)
     for off in (1, -1):
         br_send(z, off, 9)
@@ -171,14 +173,21 @@
     loads[2].wait()
     fr = fold3(mm(r3, fv[...], NT))
     columns(lambda cols: acc.__setitem__((slice(None), cols), fv[:, cols].astype(F32)))
+    ticks(AT[1])
     loads[3].wait()
-    ticks(AT[0])
-    wait_bytes(br.at[pl.ds(0, 4)], one_r.at[8])
+    wait_bytes(br.at[pl.ds(0, 2)], one_r.at[8])
+    br_send(zat(-3), 3, 10)
+    br_send(zat(3), -3, 10)
     for off in (1, -1):
-        for o in (3, -3, 6, -6):
+        for o in (3, -3):
+            br_send(zat(o), off, 9)
+    ticks(AT[2])
+    wait_bytes(br.at[pl.ds(0, 2)], one_r.at[10])
+    for off in (1, -1):
+        for o in (6, -6):
             br_send(zat(o), off, 9)
     br_send(zat(-6), 2, 9)
-    ticks(AT[1])
+    ticks(AT[3])
     wait_bytes(br.at[pl.ds(0, 11)], one_r.at[9])
     br3 = stack3(jnp.concatenate([br[i] for i in range(NZ)], axis=1))
     psend[...] = fr + fold3(mm(br3, av[...], NN))
@@ -221,9 +230,8 @@
                 device_id={"rep": to}, device_id_type=MESH,
             ).start()
 
-    ticks(AT[2])
+    ticks(AT[4])
     gather_terms([0])
-    ticks(AT[3])
     own_p = lax.rem(me, 4) == 0
 
     @pl.when(own_p)
@@ -239,8 +247,8 @@
                 device_id={"rep": lax.rem(me + d, NR)}, device_id_type=MESH,
             ).start()
 
+    ticks(AT[5])
     gather_terms([-1, 1])
-    ticks(AT[4])
 
     @pl.when(own_p)
     def _():
@@ -262,15 +270,17 @@
     packed = jnp.zeros((8, 128), F32)
     for q in range(4):
         packed = jnp.where((lane >= 32 * q) & (lane < 32 * q + 32), g[8 * q : 8 * q + 8], packed)
-    gsum[z // 4] = packed
-    z_first(gsum, 2)
-    ticks(AT[5])
+    gsum[z] = packed
+    for off in (8, 7, 9, 6, 10, 5, 11, 4, 12, 3, 13, 2, 14, 1, 15):
+        pltpu.make_async_remote_copy(
+            gsum.at[z], gsum.at[z], one_s.at[2], one_r.at[2],
+            device_id={"shard": zat(off)}, device_id_type=MESH,
+        ).start()
+    ticks(AT[6])
     gather_terms([-2, 2])
-    ticks(AT[6])
-    z_second(gsum, 2)
     ticks(AT[7])
-    l_inv = inverse_factor(z_total(gsum, 2))
-    ticks(AT[8])
+    wait_bytes(gsum.at[pl.ds(0, NZ - 1)], one_r.at[2])
+    l_inv = inverse_factor(jnp.sum(gsum[...], axis=0))
     l_hi, l_mid, l_low = split3(l_inv)
     o_t = mm(l_hi, p_hi, NN) + (
         (mm(l_hi, p_mid, NN) + mm(l_mid, p_hi, NN))
@@ -291,39 +301,45 @@
         usend[i] = fold3(mm(o3, av[block(zat(o)), :], NT))
         u_copy(i).start()
     for s in range(3, HELD + 1):
-        ticks(PARTS * s)
         gather_terms([-s, s])
+    def held_terms(cols):
+        m_hi, m_mid, _ = split3(acc[:, cols])
+        cross = mm(o3[: 2 * K], m_mid, NN)
+        wsend[:, cols] = fold3(mm(o3, m_hi, NN)) + (cross[:K] + cross[K:])
+
+    columns(held_terms)
     for i in range(len(hops)):
         u_copy(i).wait_recv()
     u_up = sum(urecv[i] for i in range(len(hops)) if hops[i][0] > 0)
     u_down = sum(urecv[i] for i in range(len(hops)) if hops[i][0] < 0)
     u3 = stack3(jnp.concatenate([u_up, u_down], axis=1))
 
-    def w_terms(cols):
-        m_hi, m_mid, _ = split3(acc[:, cols])
-        rows = jnp.concatenate([ball[block(zat(HELD)), cols], ball[block(zat(-HELD)), cols]], axis=0)
-        total = mm(o3, m_hi, NN) + mm(u3, rows, NN)
-        cross = mm(o3[: 2 * K], m_mid, NN)
-        wsend[:, cols] = fold3(total) + (cross[:K] + cross[K:])
-
-    columns(w_terms)
-
     def w_chunk(q):
         return (
             pl.ds(pl.multiple_of(lax.rem(q, 2) * 16, 16), 16),
             pl.ds(pl.multiple_of(q // 2 * 128, 128), 128),
         )
 
-    @pl.loop(0, W_OWNERS)
-    def _(q):
-        @pl.when(q != me)
-        def _():
-            pltpu.make_async_remote_copy(
-                wsend.at[w_chunk(q)], wrs.at[lax.rem(me - q + (NR - 1), NR)], one_s.at[4], one_r.at[4],
-                device_id={"rep": q}, device_id_type=MESH,
-            ).start()
-
-    ticks(AT[9])
+    def w_terms(i, width):
+        cols = pl.ds(pl.multiple_of(i * 256, 256), width)
+        rows = jnp.concatenate([ball[block(zat(HELD)), cols], ball[block(zat(-HELD)), cols]], axis=0)
+        wsend[:, cols] += fold3(mm(u3, rows, NN))
+        for j in range(width // 64):
+            q = 4 * i + j
+
+            @pl.when(q != me)
+            def _():
+                pltpu.make_async_remote_copy(
+                    wsend.at[w_chunk(q)], wrs.at[lax.rem(me - q + (NR - 1), NR)], one_s.at[4], one_r.at[4],
+                    device_id={"rep": q}, device_id_type=MESH,
+                ).start()
+
+    @pl.loop(0, 6)
+    def _(i):
+        w_terms(i, 256)
+
+    w_terms(6, 128)
+    ticks(AT[8])
     own_w = me < W_OWNERS
 
     @pl.when(own_w)
@@ -332,15 +348,14 @@
         wsum[z // 4] = jnp.sum(wrs[0 : NR - 1], axis=0) + wsend[w_chunk(me)]
         z_first(wsum, 5)
 
+    ticks(AT[9])
+    gather_terms([-5, 5])
+
+    @pl.when(own_w)
+    def _():
+        z_second(wsum, 5)
+
     ticks(AT[10])
-    gather_terms([-5, 5])
-    ticks(AT[11])
-
-    @pl.when(own_w)
-    def _():
-        z_second(wsum, 5)
-
-    ticks(AT[12])
 
     @pl.when(own_w)
     def _():
@@ -353,9 +368,9 @@
                 device_id={"rep": lax.rem(me + d, NR)}, device_id_type=MESH,
             ).start()
 
-    ticks(AT[13])
+    ticks(AT[11])
     gather_terms([-6, 6])
-    ticks(AT[14])
+    ticks(AT[12])
 
     @pl.when(own_w)
     def _():
@@ -375,9 +390,8 @@
         acc[:, cols] -= rebuilt
 
     columns(rebuild)
-    ticks(PARTS * 7)
     gather_terms([-7, 7])
-    ticks(PARTS * 8)
+    ticks(PARTS * 9)
     last = av[block(zat(8)), :].T
 
     def finish(cols):
@@ -389,12 +403,12 @@
         for way in range(2):
             if used(way, k // PARTS, k % PARTS):
                 ring(way, k // PARTS, k % PARTS).wait_send()
-    wait_bytes(br.at[pl.ds(0, 4)], one_s.at[8])
+    wait_bytes(br.at[pl.ds(0, 2)], one_s.at[8])
+    wait_bytes(br.at[pl.ds(0, 2)], one_s.at[10])
     wait_bytes(br.at[pl.ds(0, 11)], one_s.at[9])
     for i in range(len(hops)):
         u_copy(i).wait_send()
-    for i in (2, 3):
-        wait_bytes(gsum.at[pl.ds(0, 3)], one_s.at[i])
+    wait_bytes(gsum.at[pl.ds(0, NZ - 1)], one_s.at[2])
 
     @pl.when(own_p)
     def _():
@@ -452,7 +466,7 @@
             pltpu.VMEM((K, H), F32),
             pltpu.VMEM((NR, 8, 128), F32),
             pltpu.VMEM((K, H), F32),
-            pltpu.VMEM((8, 8, 128), F32),
+            pltpu.VMEM((NZ, 8, 128), F32),
             pltpu.VMEM((K, H), F32),
             pltpu.VMEM((n_hops, K, TB), F32),
             pltpu.VMEM((n_hops, K, TB), F32),
@@ -464,8 +478,8 @@
             dma((2, 8, PARTS)),
             dma((n_hops,)),
             dma((n_hops,)),
-            dma((10,)),
-            dma((10,)),
+            dma((11,)),
+            dma((11,)),
         ],
         compiler_params=pltpu.CompilerParams(
             collective_id=0, has_side_effects=True, vmem_limit_bytes=61 * 2**20

time: 110 us -> 104 us (0.945)
  Pallas kernels: 109 us -> 103 us
    pallas_call x1, Pallas kernels: 108 us -> 102 us  [on_device(): pl.pallas_call(kernel, out_shape=tuple((pltpu.VMEM(s.shape, s.dtype) for...]
where the time goes in v3:
time: 104 us
  Pallas kernels  103 us (99%)
    pallas_call x1, Pallas kernels, on_device(): pl.pallas_call(kernel, out_shape=tuple((pltpu.VMEM(s.shape, s.dtype) for...  102 us

profile of v3, /device:TPU:1, one launch (start us, length us, event | category | flops | bytes accessed | tf_op | source)
XLA Modules:
  0.0 103.9 jit_solution(17544434467072002128)
XLA Ops:
  0.6 102.0 %shard_map.67 = (bf16[256,1664]{1,0:T(8,128)(2,1)S(1)}, bf16[1,256,1664]{2,1,0:T(8,128)(2,1)S(1)}, f32[32,1664]{1,0:T(8,128)S(1)}) custom-call(bf16[1,2048,256]{2,1,0:T(8,128)(2,1)} %a_ref.1, bf16[1,128,1664]{2,1,0:T(8,128)(2,1)} %b_ref.1, bf16[1,256,1664]{2,1,0:T(8,128)(2,1)} %f_ref.1, f32[32,1664]{1,0:T(8,128)} %bitcast.2), custom_call_target="tpu_custom_call" | custom-call | flops 1744830464 | bytes 5000000 | tf_op jit(solution)/shard_map/pallas_call | solution.py:454
  102.6 1.3 %shard_map.68 = (bf16[256,1664]{1,0:T(8,128)(2,1)}, bf16[1,256,1664]{2,1,0:T(8,128)(2,1)}, f32[32,1664]{1,0:T(8,128)}) custom-call(bf16[256,1664]{1,0:T(8,128)(2,1)S(1)} %get-tuple-element.9.avg_ref, bf16[1,256,1664]{2,1,0:T(8,128)(2,1)S(1)} %get-tuple-element.10.next_ref, f32[32,1664]{1,0:T(8,128)S(1)} %get-tuple-element.11.rf_ref), custom_call_target="tpu_custom_call" | custom-call | tf_op jit(solution)/shard_map/pallas_call | solution.py:491

commit v4 on v3

--- a/solution.py
+++ b/solution.py
@@ -15,7 +15,7 @@
 NEAR = (3, -3, 2, -2, 1, -1)
 P_OWNERS = 8
 W_OWNERS = 26
-AT = (1, 2, 4, 6, 8, 11, 14, 16, 22, 25, 27, 30, 32)
+AT = (1, 2, 3, 5, 7, 10, 13, 16, 21, 24, 26, 29, 31)
 NN = (((1,), (0,)), ((), ()))
 NT = (((1,), (1,)), ((), ()))
 TN = (((0,), (0,)), ((), ()))
@@ -270,17 +270,13 @@
     packed = jnp.zeros((8, 128), F32)
     for q in range(4):
         packed = jnp.where((lane >= 32 * q) & (lane < 32 * q + 32), g[8 * q : 8 * q + 8], packed)
-    gsum[z] = packed
-    for off in (8, 7, 9, 6, 10, 5, 11, 4, 12, 3, 13, 2, 14, 1, 15):
-        pltpu.make_async_remote_copy(
-            gsum.at[z], gsum.at[z], one_s.at[2], one_r.at[2],
-            device_id={"shard": zat(off)}, device_id_type=MESH,
-        ).start()
+    gsum[z // 4] = packed
+    z_first(gsum, 2)
     ticks(AT[6])
     gather_terms([-2, 2])
+    z_second(gsum, 2)
     ticks(AT[7])
-    wait_bytes(gsum.at[pl.ds(0, NZ - 1)], one_r.at[2])
-    l_inv = inverse_factor(jnp.sum(gsum[...], axis=0))
+    l_inv = inverse_factor(z_total(gsum, 2))
     l_hi, l_mid, l_low = split3(l_inv)
     o_t = mm(l_hi, p_hi, NN) + (
         (mm(l_hi, p_mid, NN) + mm(l_mid, p_hi, NN))
@@ -408,7 +404,8 @@
     wait_bytes(br.at[pl.ds(0, 11)], one_s.at[9])
     for i in range(len(hops)):
         u_copy(i).wait_send()
-    wait_bytes(gsum.at[pl.ds(0, NZ - 1)], one_s.at[2])
+    for i in (2, 3):
+        wait_bytes(gsum.at[pl.ds(0, 3)], one_s.at[i])
 
     @pl.when(own_p)
     def _():
@@ -466,7 +463,7 @@
             pltpu.VMEM((K, H), F32),
             pltpu.VMEM((NR, 8, 128), F32),
             pltpu.VMEM((K, H), F32),
-            pltpu.VMEM((NZ, 8, 128), F32),
+            pltpu.VMEM((8, 8, 128), F32),
             pltpu.VMEM((K, H), F32),
             pltpu.VMEM((n_hops, K, TB), F32),
             pltpu.VMEM((n_hops, K, TB), F32),

time: 104 us -> 102 us (0.981)
  Pallas kernels: 103 us -> 101 us
    pallas_call x1, Pallas kernels: 102 us -> 99.6 us  [on_device(): pl.pallas_call(kernel, out_shape=tuple((pltpu.VMEM(s.shape, s.dtype) for...]
where the time goes in v4:
time: 102 us; the launch traced here: 101 us
  Pallas kernels  101 us (99%)
    pallas_call x1, Pallas kernels, on_device(): pl.pallas_call(kernel, out_shape=tuple((pltpu.VMEM(s.shape, s.dtype) for...  99.6 us

profile of v4, /device:TPU:1, one launch (start us, length us, event | category | flops | bytes accessed | tf_op | source)
XLA Modules:
  0.0 101.5 jit_solution(11072416472494074229)
XLA Ops:
  0.6 99.6 %shard_map.67 = (bf16[256,1664]{1,0:T(8,128)(2,1)S(1)}, bf16[1,256,1664]{2,1,0:T(8,128)(2,1)S(1)}, f32[32,1664]{1,0:T(8,128)S(1)}) custom-call(bf16[1,2048,256]{2,1,0:T(8,128)(2,1)} %a_ref.1, bf16[1,128,1664]{2,1,0:T(8,128)(2,1)} %b_ref.1, bf16[1,256,1664]{2,1,0:T(8,128)(2,1)} %f_ref.1, f32[32,1664]{1,0:T(8,128)} %bitcast.2), custom_call_target="tpu_custom_call" | custom-call | flops 1744830464 | bytes 5000000 | tf_op jit(solution)/shard_map/pallas_call | solution.py:451
  100.2 1.3 %shard_map.68 = (bf16[256,1664]{1,0:T(8,128)(2,1)}, bf16[1,256,1664]{2,1,0:T(8,128)(2,1)}, f32[32,1664]{1,0:T(8,128)}) custom-call(bf16[256,1664]{1,0:T(8,128)(2,1)S(1)} %get-tuple-element.9.avg_ref, bf16[1,256,1664]{2,1,0:T(8,128)(2,1)S(1)} %get-tuple-element.10.next_ref, f32[32,1664]{1,0:T(8,128)S(1)} %get-tuple-element.11.rf_ref), custom_call_target="tpu_custom_call" | custom-call | tf_op jit(solution)/shard_map/pallas_call | solution.py:488

commit v5 on v4

--- a/solution.py
+++ b/solution.py
@@ -193,7 +193,7 @@
     psend[...] = fr + fold3(mm(br3, av[...], NN))
 
     def z_first(ref, i):
-        for off in (4, 8, 12):
+        for off in (8, 4, 12):
             pltpu.make_async_remote_copy(
                 ref.at[z // 4], ref.at[z // 4], one_s.at[i], one_r.at[i],
                 device_id={"shard": zat(off)}, device_id_type=MESH,
@@ -203,7 +203,7 @@
         wait_bytes(ref.at[pl.ds(0, 3)], one_r.at[i])
         mine = 4 + lax.rem(z, 4)
         ref[mine] = (ref[0] + ref[1]) + (ref[2] + ref[3])
-        for off in (1, 2, -1):
+        for off in (2, 1, -1):
             pltpu.make_async_remote_copy(
                 ref.at[mine], ref.at[mine], one_s.at[i + 1], one_r.at[i + 1],
                 device_id={"shard": zat(off)}, device_id_type=MESH,
@@ -286,6 +286,7 @@
     o3 = stack3(o_t)
 
     hops = [(o, o - HELD) for o in range(HELD + 1, 9)] + [(-o, HELD - o) for o in range(HELD + 1, 8)]
+    hops.sort(key=lambda hop: -abs(hop[1]))
 
     def u_copy(i):
         return pltpu.make_async_remote_copy(

time: 102 us -> 101 us (level)
  no operation moved by 1% of the time
where the time goes in v5:
time: 101 us
  Pallas kernels  101 us (100%)
    pallas_call x1, Pallas kernels, on_device(): pl.pallas_call(kernel, out_shape=tuple((pltpu.VMEM(s.shape, s.dtype) for...  99.4 us

profile of v5, /device:TPU:1, one launch (start us, length us, event | category | flops | bytes accessed | tf_op | source)
XLA Modules:
  0.0 101.3 jit_solution(4517619549829324241)
XLA Ops:
  0.6 99.4 %shard_map.67 = (bf16[256,1664]{1,0:T(8,128)(2,1)S(1)}, bf16[1,256,1664]{2,1,0:T(8,128)(2,1)S(1)}, f32[32,1664]{1,0:T(8,128)S(1)}) custom-call(bf16[1,2048,256]{2,1,0:T(8,128)(2,1)} %a_ref.1, bf16[1,128,1664]{2,1,0:T(8,128)(2,1)} %b_ref.1, bf16[1,256,1664]{2,1,0:T(8,128)(2,1)} %f_ref.1, f32[32,1664]{1,0:T(8,128)} %bitcast.2), custom_call_target="tpu_custom_call" | custom-call | flops 1744830464 | bytes 5000000 | tf_op jit(solution)/shard_map/pallas_call | solution.py:452
  100.0 1.3 %shard_map.68 = (bf16[256,1664]{1,0:T(8,128)(2,1)}, bf16[1,256,1664]{2,1,0:T(8,128)(2,1)}, f32[32,1664]{1,0:T(8,128)}) custom-call(bf16[256,1664]{1,0:T(8,128)(2,1)S(1)} %get-tuple-element.9.avg_ref, bf16[1,256,1664]{2,1,0:T(8,128)(2,1)S(1)} %get-tuple-element.10.next_ref, f32[32,1664]{1,0:T(8,128)S(1)} %get-tuple-element.11.rf_ref), custom_call_target="tpu_custom_call" | custom-call | tf_op jit(solution)/shard_map/pallas_call | solution.py:489
